TPU v7x, 32 devices: a whole 2x2x4 slice. The times are simulated.
32 devices in a mesh: groups: 2 (over x), out: 16 (over z, y, core).
Axes of the slice: x: 2, y: 2, z: 4, core: 2. Of those that a mesh axis runs over, the one named last changes fastest.
Arguments:
- stream: bfloat16 [128, 12288], P('groups', 'out'), parts along dimension 0, may hold values from -6 to 6
- norm_gain: float32 [12288], replicated, may hold values from 0.5 to 1.5
- w_query: bfloat16 [12288, 6144], P(None, 'out')
- w_keyval: bfloat16 [12288, 1024], P(None, 'out'), may hold values from -0.0546875 to 0.0546875
- w_out: bfloat16 [6144, 12288], P('out'), may hold values from -0.75 to 0.75
- lengths: int32 [128], P(('groups', 'out')), parts along dimension 0, may hold values from 1 to 512, as said below
- key_cache: bfloat16 [128, 512, 512], P(('groups', 'out')), parts along dimension 0, may hold values from -127 to 127, as said below
- value_cache: bfloat16 [128, 512, 512], P(('groups', 'out')), parts along dimension 0, may hold values from -127 to 127, as said below
- key_scales: int32 [128, 4, 4], P(('groups', 'out')), parts along dimension 0, may hold values from -8 to -6
- value_scales: int32 [128, 4, 4], P(('groups', 'out')), parts along dimension 0, may hold values from -8 to -6
Outputs:
- new_stream: bfloat16 [128, 12288], P('groups', 'out'), parts along dimension 0
There are 2 independent parts, one for each index of `groups`. A program takes and returns all parts, laid end to end along the dimension named above; an argument that names none is the same for every part. Nothing has to cross between parts.
Inputs may be any that keep to these rules, and one draw needn't show every extreme that they name: `lengths`: every row holds at least one earlier token; in every draw some row holds exactly 512. `key_cache`: whole numbers, codes of an eight-bit cache. `value_cache`: whole numbers, codes of an eight-bit cache.
All inputs are finite; a program needn't handle non-finite values.
Results may differ from a plain program's by a relative error of at most 0.024.
The roundings to bfloat16 on the way count: a program that leaves them out, or rounds other values in their place, can miss the bound.
Values may be sent and summed in bfloat16 or wider, within the bound.
A program may use at most 64 MiB of HBM per device.

v0:
```python
import math

import jax
import jax.numpy as jnp
from jax import lax
from jax.sharding import PartitionSpec as P

HQ = 48
KVH = 4
HD = 128


rope_base = 1000000.0
norm_eps = 1e-05


def rotate(vec, position):
    half = vec.shape[-1] // 2
    index = jnp.arange(half, dtype=jnp.float32)
    freq = jnp.exp(index * (-2.0 * math.log(rope_base) / vec.shape[-1]))
    angle = position * freq
    cosine = jnp.cos(angle)
    sine = jnp.sin(angle)
    first = vec[..., :half]
    second = vec[..., half:]
    return jnp.concatenate(
        [first * cosine - second * sine, second * cosine + first * sine], axis=-1
    )


def dequant(cache, scales):
    rows, span, width = cache.shape
    blocks = scales.shape[1]
    factor = jnp.exp2(scales.astype(jnp.float32)).astype(jnp.bfloat16)
    shaped = cache.reshape(rows, blocks, span // blocks, KVH, width // KVH)
    return (shaped * factor[:, :, None, :, None]).reshape(rows, span, KVH, width // KVH)


def per_device(
    stream,
    norm_gain,
    w_query,
    w_keyval,
    w_out,
    lengths,
    key_cache,
    value_cache,
    key_scales,
    value_scales,
):
    local_rows = lengths.shape[0]
    xf = stream.astype(jnp.float32)
    whole = lax.all_gather(stream, "out", axis=1, tiled=True).astype(jnp.float32)
    meansq = jnp.mean(whole * whole, axis=-1, keepdims=True)
    normed = (whole * lax.rsqrt(meansq + norm_eps) * norm_gain).astype(jnp.bfloat16)
    q_local = jnp.dot(normed, w_query, preferred_element_type=jnp.float32).astype(jnp.bfloat16)
    kv_local = jnp.dot(normed, w_keyval, preferred_element_type=jnp.float32).astype(jnp.bfloat16)
    q_rows, kv_rows = (
        lax.all_to_all(q_local, "out", split_axis=0, concat_axis=1, tiled=True),
        lax.all_to_all(kv_local, "out", split_axis=0, concat_axis=1, tiled=True),
    )
    position = lengths.astype(jnp.float32)[:, None, None]
    rotated = rotate(q_rows.astype(jnp.float32).reshape(local_rows, HQ, HD), position).astype(
        jnp.bfloat16
    )
    rotated = rotated.reshape(local_rows, KVH, HQ // KVH, HD)
    new_key = rotate(
        kv_rows[:, : KVH * HD].astype(jnp.float32).reshape(local_rows, KVH, HD), position
    ).astype(jnp.bfloat16)
    new_value = kv_rows[:, KVH * HD :].reshape(local_rows, KVH, HD)
    factor = HD ** (-0.5)
    own = jnp.einsum("rkgd,rkd->rkg", rotated, new_key, preferred_element_type=jnp.float32) * factor
    span = key_cache.shape[1]
    scores = (
        jnp.einsum(
            "rkgd,rjkd->rkgj",
            rotated,
            dequant(key_cache, key_scales),
            preferred_element_type=jnp.float32,
        )
        * factor
    )
    valid = jnp.arange(span, dtype=jnp.int32)[None, :] < lengths[:, None]
    scores = jnp.where(valid[:, None, None, :], scores, -jnp.inf)
    top = jnp.maximum(jnp.max(scores, axis=-1), own)
    weights = jnp.exp(scores - top[..., None])
    own_weight = jnp.exp(own - top)
    total = jnp.sum(weights, axis=-1) + own_weight
    own_rounded = lax.optimization_barrier(own_weight.astype(jnp.bfloat16)).astype(jnp.float32)
    summed = jnp.einsum(
        "rkgj,rjkd->rkgd",
        weights.astype(jnp.bfloat16),
        dequant(value_cache, value_scales),
        preferred_element_type=jnp.float32,
    )
    summed = summed + own_rounded[..., None] * new_value.astype(jnp.float32)[:, :, None, :]
    attended = (summed / total[..., None]).astype(jnp.bfloat16).reshape(local_rows, HQ * HD)
    heads = lax.all_to_all(attended, "out", split_axis=1, concat_axis=0, tiled=True)
    partial_terms = jnp.dot(heads, w_out, preferred_element_type=jnp.float32)
    projected = lax.psum_scatter(partial_terms, "out", scatter_dimension=1, tiled=True)
    return (xf + projected).astype(jnp.bfloat16)


def solution(mesh):
    return jax.shard_map(
        per_device,
        mesh=mesh,
        in_specs=(
            P("groups", "out"),
            P(),
            P(None, "out"),
            P(None, "out"),
            P("out", None),
            P(("groups", "out")),
            P(("groups", "out"), None, None),
            P(("groups", "out"), None, None),
            P(("groups", "out"), None, None),
            P(("groups", "out"), None, None),
        ),
        out_specs=P("groups", "out"),
        check_vma=False,
    )
```

profile of v0, /device:TPU:0, one launch (start us, length us, event | category | flops | bytes accessed | tf_op | source)
XLA Modules:
  0.0 173.6 jit_solution(13237535919706573012)
XLA Ops:
  6.5 0.0 copy-start
  6.5 0.0 all-gather.2.cloned.1.call-start
  6.5 0.7 all-gather.2.cloned.1.call-update
  7.3 0.7 convert_element_type.76
  7.9 0.7 exponential_convert_fusion.1
  8.6 0.1 copy.31
  8.8 0.7 exponential_convert_fusion
  9.5 0.1 copy.34
  9.6 0.1 mul.191
  9.7 0.1 mul.177
  9.8 0.7 iota_compare_fusion
  10.6 0.1 multiply_cosine_fusion
  10.7 41.3 %all-gather.2.cloned.1.call-done = bf16[64,12288]{1,0:T(8,128)(2,1)} async-done(((bf16[64,768]{1,0:T(8,128)(2,1)}), bf16[64,12288]{1,0:T(8,128)(2,1)}) %all-gather.2.cloned.1.call-update) | async-done | bytes 1572880 | tf_op jit(solution)/shard_map/all_gather | solution.py:53
  52.0 1.8 %fusion = f32[64]{0:T(128)S(1)} fusion(bf16[64,12288]{1,0:T(8,128)(2,1)} %all-gather.2.cloned.1.call-done), kind=kLoop, calls=%fused_computation.2 | loop fusion | flops 2359232 | bytes 1573120 | tf_op jit(solution)/shard_map/reduce_sum | solution.py:54
  53.8 0.0 copy-start.2
  53.8 2.6 %convolution_convert_fusion.1 = bf16[64,64]{1,0:T(8,128)(2,1)S(1)} fusion(bf16[12288,64]{0,1:T(8,128)(2,1)} %param.13, bf16[64,12288]{1,0:T(8,128)(2,1)} %all-gather.2.cloned.1.call-done, f32[12288]{0:T(1024)} %param.11, f32[64]{0:T(128)S(1)} %add_rsqrt_fusion), kind=kOutput, calls=%fused_computation.17 | convolution fusion | flops 103813120 | bytes 3203328 | tf_op jit(solution)/shard_map/dot_general | solution.py:57
  56.4 0.7 reshape.147
  57.1 3.7 %all-to-all-start.1 = ((bf16[16,2,128]{2,1,0:T(2,128)(2,1)}), bf16[16,2,128]{2,1,0:T(2,128)(2,1)S(1)}, u32[]{:S(2)}, u32[]{:S(2)}) async-start(bf16[16,2,128]{2,1,0:T(2,128)(2,1)} %reshape.147), calls=%async_computation.1 | async-start | bytes 16384 | tf_op jit(solution)/shard_map/all_to_all | solution.py:60
  60.8 0.0 copy-done.2
  60.8 5.8 %convolution_convert_fusion = bf16[64,384]{1,0:T(8,128)(2,1)S(1)} fusion(bf16[12288,384]{1,0:T(8,128)(2,1)} %param.12, bf16[64,12288]{1,0:T(8,128)(2,1)} %all-gather.2.cloned.1.call-done, f32[12288]{0:T(1024)S(1)} %copy-done.2, f32[64]{0:T(128)S(1)} %add_rsqrt_fusion), kind=kOutput, calls=%fused_computation.16 | convolution fusion | flops 607150080 | bytes 11108608 | tf_op jit(solution)/shard_map/dot_general | solution.py:56
  66.7 0.6 all_to_all.38
  67.3 0.0 all-to-all-done.1
  67.3 6.0 %all-to-all-start = ((bf16[16,4,384]{2,1,0:T(4,128)(2,1)}), bf16[16,4,384]{2,1,0:T(4,128)(2,1)S(1)}, u32[]{:S(2)}, u32[]{:S(2)}) async-start(bf16[16,4,384]{2,1,0:T(4,128)(2,1)} %all_to_all.38), calls=%async_computation | async-start | bytes 98304 | tf_op jit(solution)/shard_map/all_to_all | solution.py:59
  73.4 0.0 reduce-scatter.2.cloned.1.call-start
  73.4 0.1 reshape.148
  73.5 0.1 all_to_all.43
  73.6 0.1 subtract_convert_fusion.1
  73.7 0.1 maximum_bitcast_fusion
  73.8 6.3 %all-to-all-done = bf16[16,4,384]{2,1,0:T(4,128)(2,1)S(1)} async-done(((bf16[16,4,384]{2,1,0:T(4,128)(2,1)}), bf16[16,4,384]{2,1,0:T(4,128)(2,1)S(1)}, u32[]{:S(2)}, u32[]{:S(2)}) %all-to-all-start) | async-done | bytes 49184 | tf_op jit(solution)/shard_map/all_to_all | solution.py:59
  80.2 0.1 subtract_convert_fusion
  80.4 0.2 fusion.20
  80.6 0.0 copy-done
  80.6 0.0 copy-start.3
  80.6 2.2 %fusion.26 = (f32[4,4,12]{2,1,0:T(4,128)S(1)}, f32[4,4,12,512]{3,2,1,0:T(8,128)S(1)}) fusion(bf16[4,512,4]{1,2,0:T(4,128)(2,1)S(1)} %mul.178, bf16[4,4,12,64]{3,2,1,0:T(8,128)(2,1)S(1)} %copy.30, bf16[4,4,12,64]{3,2,1,0:T(8,128)(2,1)S(1)} %copy.29, pred[4,512]{1,0:T(4,128)(4,1)S(1)} %iota_compare_fusion, bf16[4,512,512]{2,1,0:T(8,128)(2,1)S(1)} %copy-done), kind=kOutput, calls=%fused_computation.49 | convolution fusion | flops 29753152 | bytes 2558720 | tf_op jit(solution)/shard_map/rkgd,rjkd->rkgj/dot_general | solution.py:75
  82.8 0.3 fusion.14
  83.1 0.0 copy-done.3
  83.1 1.9 %fusion.11 = bf16[4,4,12,128]{3,2,1,0:T(8,128)(2,1)S(1)} fusion(bf16[4,512,4]{1,2,0:T(4,128)(2,1)S(1)} %mul.192, f32[4,4,12,512]{3,2,1,0:T(8,128)S(1)} %get-tuple-element.16, f32[4,4,12]{2,1,0:T(4,128)S(1)} %multiply_maximum_fusion, f32[4,4,12]{2,1,0:T(4,128)S(1)} %get-tuple-element.8, f32[4,4,128]{2,1,0:T(4,128)S(1)} %reshape.143, ...), kind=kOutput, calls=%fused_computation.15 | convolution fusion | flops 29655040 | bytes 2566400 | tf_op jit(solution)/shard_map/rkgj,rjkd->rkgd/dot_general | solution.py:90
  85.1 9.3 %all_to_all.51 = bf16[4,16,384]{2,0,1:T(4,128)(2,1)S(1)} all-to-all(bf16[4,16,384]{2,0,1:T(4,128)(2,1)S(1)} %copy.36), channel_id=1, replica_groups=mesh['groups'=2,'out'=16] {'out'}, dimensions={1} | all-to-all | bytes 98304 | tf_op jit(solution)/shard_map/all_to_all | solution.py:98
  94.5 7.1 %fusion.27 = f32[64,12288]{1,0:T(8,128)} fusion(bf16[64,384]{1,0:T(8,128)(2,1)S(1)} %all_to_all.47, bf16[384,12288]{1,0:T(8,128)(2,1)} %param.14), kind=kOutput, calls=%fused_computation.50 | convolution fusion | flops 603979776 | bytes 12632064 | tf_op jit(solution)/shard_map/dot_general | solution.py:99
  101.6 0.0 copy-start.1
  101.6 0.0 reduce-scatter.2.cloned.1.call-update
  101.6 63.6 %reduce-scatter.2.cloned.1.call-done = f32[64,768]{1,0:T(8,128)} async-done(((f32[64,12288]{1,0:T(8,128)}), f32[64,768]{1,0:T(8,128)}) %reduce-scatter.2.cloned.1.call-update) | async-done | bytes 196624 | tf_op jit(solution)/shard_map/reduce_scatter | solution.py:100
  165.2 0.0 copy-done.1
  165.2 1.6 add_convert_fusion
  (21 shorter events, 0.3 us)
Async XLA Ops:
  6.5 74.1 %copy-start = (bf16[4,512,512]{2,1,0:T(8,128)(2,1)S(1)}, bf16[4,512,512]{2,1,0:T(8,128)(2,1)}, u32[]{:S(2)}) copy-start(bf16[4,512,512]{2,1,0:T(8,128)(2,1)} %param.16) | copy-start | bytes 6291460
  6.5 45.4 %all-gather.2.cloned.1.call-start = ((), (), s32[]{:S(2)}) async-start(), calls=%async_computation.4 | async-start | bytes 1671168 | tf_op jit(solution)/shard_map/all_gather | solution.py:53
  53.8 7.0 %copy-start.2 = (f32[12288]{0:T(1024)S(1)}, f32[12288]{0:T(1024)}, u32[]{:S(2)}) copy-start(f32[12288]{0:T(1024)} %param.11) | copy-start | bytes 147460
  57.1 10.3 %all-to-all-start.1 = ((bf16[16,2,128]{2,1,0:T(2,128)(2,1)}), bf16[16,2,128]{2,1,0:T(2,128)(2,1)S(1)}, u32[]{:S(2)}, u32[]{:S(2)}) async-start(bf16[16,2,128]{2,1,0:T(2,128)(2,1)} %reshape.147), calls=%async_computation.1 | async-start | bytes 16384 | tf_op jit(solution)/shard_map/all_to_all | solution.py:60
  67.3 12.8 %all-to-all-start = ((bf16[16,4,384]{2,1,0:T(4,128)(2,1)}), bf16[16,4,384]{2,1,0:T(4,128)(2,1)S(1)}, u32[]{:S(2)}, u32[]{:S(2)}) async-start(bf16[16,4,384]{2,1,0:T(4,128)(2,1)} %all_to_all.38), calls=%async_computation | async-start | bytes 98304 | tf_op jit(solution)/shard_map/all_to_all | solution.py:59
  73.4 91.9 %reduce-scatter.2.cloned.1.call-start = ((), (), s32[]{:S(2)}) async-start(), calls=%async_computation.5 | async-start | bytes 3342336 | tf_op jit(solution)/shard_map/reduce_scatter | solution.py:100
  80.6 2.5 %copy-start.3 = (bf16[4,512,512]{2,1,0:T(8,128)(2,1)S(1)}, bf16[4,512,512]{2,1,0:T(8,128)(2,1)}, u32[]{:S(2)}) copy-start(bf16[4,512,512]{2,1,0:T(8,128)(2,1)} %param.17) | copy-start | bytes 6291460
  101.6 63.6 %copy-start.1 = (bf16[64,768]{1,0:T(8,128)(2,1)S(1)}, bf16[64,768]{1,0:T(8,128)(2,1)}, u32[]{:S(2)}) copy-start(bf16[64,768]{1,0:T(8,128)(2,1)} %param.10) | copy-start | bytes 294916
Sparse Core Ops, SparseCore 0:
  9.6 42.3 all-gather.1
  101.7 63.4 reduce-scatter.1
where the time goes:
time: 174 us
  waiting for transfers between devices  112 us (64%)
  matrix products  19.8 us (11%)
  between operations  13.6 us (8%)
  starting transfers between devices  9.79 us (6%)
  blocking collectives  9.34 us (5%)
  other arithmetic  6.88 us (4%)
  local copies, waits for them, and re-layouts  2.16 us (1%)
    reduce_scatter x1, waiting for transfers between devices, per_device(): lax.psum_scatter(partial_terms, 'out', scatter_dimension=1, tiled=True)  63.6 us
    all_gather x1, waiting for transfers between devices, per_device(): lax.all_gather(stream, 'out', axis=1, tiled=True).astype(jnp.float32)  41.3 us
    all_to_all x1, blocking collectives, per_device(): lax.all_to_all(attended, 'out', split_axis=1, concat_axis=0, tiled=True)  9.34 us
    dot_general x1, matrix products, per_device(): partial_terms = jnp.dot(heads, w_out, preferred_element_type=jnp.float32)  7.11 us
    all_to_all x1, waiting for transfers between devices, per_device(): lax.all_to_all(q_local, 'out', split_axis=0, concat_axis=1, tiled=True)  6.33 us
    all_to_all x1, starting transfers between devices, per_device(): lax.all_to_all(q_local, 'out', split_axis=0, concat_axis=1, tiled=True)  6.01 us
    dot_general x1, matrix products, per_device(): jnp.dot(normed, w_query, preferred_element_type=jnp.float32)  5.85 us
    all_to_all x1, starting transfers between devices, per_device(): lax.all_to_all(kv_local, 'out', split_axis=0, concat_axis=1, tiled=True)  3.74 us
  transfers between devices with their start and end apart: 4, of which 3 were waited for; matrix products, arithmetic and copies ran while one was open for 5% of the time, Pallas kernels for 0%

commit v1 on v0

--- a/solution.py
+++ b/solution.py
@@ -1,8 +1,11 @@
+import functools
 import math
 
 import jax
 import jax.numpy as jnp
 from jax import lax
+from jax.experimental import pallas as pl
+from jax.experimental.pallas import tpu as pltpu
 from jax.sharding import PartitionSpec as P
 
 HQ = 48
@@ -36,7 +39,7 @@
     return (shaped * factor[:, :, None, :, None]).reshape(rows, span, KVH, width // KVH)
 
 
-def per_device(
+def plain_device(
     stream,
     norm_gain,
     w_query,
@@ -101,9 +104,475 @@
     return (xf + projected).astype(jnp.bfloat16)
 
 
+MESH = pl.DeviceIdType.MESH
+F32 = jnp.float32
+BF16 = jnp.bfloat16
+CONTRACT_LAST = (((1,), (1,)), ((), ()))
+
+
+def fused_kernel(
+    n, rows, width, local_rows, span,
+    x_ref, gain_ref, cos_ref, sin_ref, len_ref, kfac_ref, vfac_ref,
+    wq_hbm, wkv_hbm, wo_hbm, kc_hbm, vc_hbm,
+    out_ref,
+    wq, wkv, wo, kc, vc, xbuf, ssend, sbuf, accq, acckv, pk, qsend, qbuf, asend, abuf, heads,
+    core_sb, core_rb, y_sb, y_rb, z_sb, up_rb, dn_rb, heads_sum,
+    wq_sem, wo_sem, w_sem,
+    ag_recv, ag_up, ag_dn, ag_y, ag_core,
+    ss_send, ss_recv, q_send, q_recv, a_send, a_recv,
+    core_send, core_recv, y_send, y_recv, z_send, up_recv, dn_recv,
+):
+    line = n // 4
+    qcols = wq.shape[1]
+    own_heads = qcols // HD
+    tile = qbuf.shape[1]
+    per_head = n // KVH
+    qrows = per_head * tile
+    me = lax.axis_index("out")
+    grp = lax.axis_index("groups")
+    a = me // 4
+    b = (me // 2) % 2
+    c = me % 2
+
+    def at(pos, bb, cc):
+        return (pos * 2 + bb) * 2 + cc
+
+    up, down = at(a + 1, b, c), at(a - 1, b, c)
+    ypeer, cpeer = at(a, 1 - b, c), at(a, b, 1 - c)
+    low, high = a, line - 1 - a
+    least = jnp.minimum(low, high)
+
+    def ranked(m):
+        d = (m + 1) // 2
+        near = jnp.where(m % 2 == 1, a - d, a + d)
+        far = jnp.where(high > low, a + (m - least), a - (m - least))
+        return jnp.where(m <= 2 * least, near, far)
+
+    def remote(src, dst, ssem, rsem, to):
+        return pltpu.make_async_remote_copy(
+            src_ref=src, dst_ref=dst, send_sem=ssem, recv_sem=rsem,
+            device_id=(grp, to), device_id_type=MESH,
+        )
+
+    def wq_copy(i):
+        at_rows = pl.ds(pl.multiple_of(i * width, width), width)
+        return pltpu.make_async_copy(wq_hbm.at[at_rows], wq.at[at_rows], wq_sem.at[i])
+
+    wo_parts = wo_sem.shape[0]
+    wo_rows = wo.shape[0] // wo_parts
+
+    def wo_copy(i):
+        at_rows = pl.ds(i * wo_rows, wo_rows)
+        return pltpu.make_async_copy(wo_hbm.at[at_rows], wo.at[at_rows], wo_sem.at[i])
+
+    wkv_copy = pltpu.make_async_copy(wkv_hbm, wkv, w_sem.at[0])
+    kc_copy = pltpu.make_async_copy(kc_hbm, kc, w_sem.at[1])
+    vc_copy = pltpu.make_async_copy(vc_hbm, vc, w_sem.at[2])
+
+    barrier = pltpu.get_barrier_semaphore()
+
+    def others(body):
+        def step(i, carry):
+            body(lax.rem(me + i, n))
+            return carry
+        lax.fori_loop(1, n, step, 0)
+
+    others(lambda o: pl.semaphore_signal(barrier, inc=1, device_id=(grp, o), device_id_type=MESH))
+
+    wkv_copy.start()
+
+    def start_wq(i, carry):
+        wq_copy(lax.rem(me + i, n)).start()
+        return carry
+    lax.fori_loop(0, n, start_wq, 0)
+    kc_copy.start()
+    vc_copy.start()
+    for i in range(wo_parts):
+        wo_copy(i).start()
+
+    xbuf[me] = x_ref[...]
+    xf = x_ref[...].astype(F32)
+    square = jnp.sum(xf * xf, axis=1, keepdims=True)
+    spread = jnp.transpose(jnp.broadcast_to(square, (rows, 128)))
+    ssend[...] = jnp.zeros_like(ssend)
+    ssend[:, 0:rows] = spread[0:8, :]
+    sbuf[me] = ssend[...]
+    accq[...] = jnp.zeros_like(accq)
+    acckv[...] = jnp.zeros_like(acckv)
+
+    pl.semaphore_wait(barrier, n - 1)
+
+    def ag_copy(block, ssem, to):
+        return remote(xbuf.at[block], xbuf.at[block], ssem, ag_recv.at[block], to)
+
+    def ag_wait(block):
+        ag_copy(block, ag_core.at[0], cpeer).wait_recv()
+
+    def spread_line(pos):
+        block = at(pos, b, c)
+
+        @pl.when((pos <= a) & (a < line - 1))
+        def _():
+            ag_copy(block, ag_up.at[pos], up).start()
+
+        @pl.when((pos >= a) & (a > 0))
+        def _():
+            ag_copy(block, ag_dn.at[pos], down).start()
+
+        ag_copy(block, ag_y.at[pos], ypeer).start()
+        ag_copy(block, ag_core.at[pos], cpeer).start()
+
+    def ss_copy(o, slot):
+        return remote(ssend, sbuf.at[slot], ss_send.at[o], ss_recv.at[slot], o)
+
+    others(lambda o: ss_copy(o, me).start())
+    spread_line(a)
+    others(lambda o: ss_copy(o, o).wait_recv())
+    total_sq = jnp.sum(sbuf[...], axis=0)[0:1, :]
+    column = jnp.transpose(jnp.broadcast_to(total_sq, (128, 128)))[0:rows, 0:1]
+    scale = lax.rsqrt(column * (1.0 / (n * width)) + norm_eps)
+    wkv_copy.wait()
+
+    def project(block):
+        wq_copy(block).wait()
+        start = pl.multiple_of(block * width, width)
+        normed = (xbuf[block].astype(F32) * scale * gain_ref[:, pl.ds(start, width)]).astype(BF16)
+        accq[...] += jnp.dot(normed, wq[pl.ds(start, width), :], preferred_element_type=F32)
+        acckv[...] += lax.dot_general(
+            normed, wkv[:, pl.ds(start, width)], CONTRACT_LAST, preferred_element_type=F32
+        )
+
+    project(me)
+
+    def gather_step(m, carry):
+        @pl.when(m < line)
+        def _():
+            pos = ranked(m)
+            ag_wait(at(pos, b, c))
+            spread_line(pos)
+
+        prev = ranked(m - 1)
+        yblock = at(prev, 1 - b, c)
+        ag_wait(yblock)
+        ag_copy(yblock, ag_core.at[line + prev], cpeer).start()
+
+        @pl.when(m < line)
+        def _():
+            project(at(ranked(m), b, c))
+
+        project(yblock)
+        cblock = at(prev, b, 1 - c)
+        ag_wait(cblock)
+        project(cblock)
+        return carry
+    lax.fori_loop(1, line + 1, gather_step, 0)
+
+    def gather_last(m, carry):
+        block = at(ranked(m), 1 - b, 1 - c)
+        ag_wait(block)
+        project(block)
+        return carry
+    lax.fori_loop(0, line, gather_last, 0)
+
+    kv_cols = wkv.shape[0]
+    pk[...] = jnp.zeros_like(pk)
+    q_all = accq[...]
+    kv_all = acckv[...]
+    for j in range(n):
+        mine = slice(j * local_rows, (j + 1) * local_rows)
+        for g in range(own_heads):
+            pk[j, g * local_rows:(g + 1) * local_rows, :] = q_all[mine, g * HD:(g + 1) * HD]
+        pk[j, own_heads * local_rows:tile, 0:kv_cols] = kv_all[mine, :]
+    qsend[...] = pk[...].astype(BF16)
+
+    def q_copy(o, slot):
+        return remote(qsend.at[o], qbuf.at[slot], q_send.at[o], q_recv.at[slot], o)
+
+    others(lambda o: q_copy(o, me).start())
+    qbuf[me] = qsend[me]
+
+    ridx = lax.broadcasted_iota(jnp.int32, (qrows, 128), 0) % local_rows
+    pick = lax.broadcasted_iota(jnp.int32, (qrows, tile), 0) % local_rows
+    pick = pick + own_heads * local_rows == lax.broadcasted_iota(jnp.int32, (qrows, tile), 1)
+    pick = pick.astype(F32).astype(BF16)
+    blocks = span // 128
+
+    def by_row(values):
+        res = jnp.full((qrows, 128), values[0])
+        for r in range(1, local_rows):
+            res = jnp.where(ridx == r, values[r], res)
+        return res
+
+    limit = by_row([len_ref[r] for r in range(local_rows)])
+    lane = lax.broadcasted_iota(jnp.int32, (qrows, 128), 1)
+    cosine, sine = cos_ref[...], sin_ref[...]
+
+    def rotated(v):
+        return (v * cosine + pltpu.roll(v, HD // 2, 1) * sine).astype(BF16)
+
+    kc_copy.wait()
+    vc_copy.wait()
+    others(lambda o: q_copy(o, o).wait_recv())
+
+    pieces = HD // kv_cols
+    factor = HD ** (-0.5)
+
+    def new_head(first):
+        res = None
+        for p in range(pieces):
+            part = jnp.dot(pick, qbuf[first + p], preferred_element_type=F32)
+            part = part if p == 0 else pltpu.roll(part, p * kv_cols, 1)
+            res = part if res is None else res + part
+        return res
+
+    for k in range(KVH):
+        at_k = slice(k * HD, (k + 1) * HD)
+        query = rotated(qbuf[k * per_head:(k + 1) * per_head].astype(F32).reshape(qrows, HD))
+        new_key = rotated(new_head(k * pieces)).astype(F32)
+        new_value = new_head((KVH + k) * pieces)
+        own = jnp.sum(query.astype(F32) * new_key, axis=1, keepdims=True) * factor
+        score = None
+        for r in range(local_rows):
+            one = lax.dot_general(query, kc[r, :, at_k], CONTRACT_LAST, preferred_element_type=F32)
+            cut = [one[:, 128 * u:128 * (u + 1)] for u in range(blocks)]
+            score = cut if r == 0 else [jnp.where(ridx == r, x, y) for x, y in zip(cut, score)]
+        top = own
+        for u in range(blocks):
+            scales = by_row([kfac_ref[(r * blocks + u) * KVH + k] for r in range(local_rows)])
+            score[u] = jnp.where(lane + 128 * u < limit, score[u] * scales * factor, -jnp.inf)
+            top = jnp.maximum(top, jnp.max(score[u], axis=1, keepdims=True))
+        own_weight = jnp.exp(own - top)
+        total = own_weight
+        weights = []
+        for u in range(blocks):
+            weight = jnp.exp(score[u] - top)
+            total = total + jnp.sum(weight, axis=1, keepdims=True)
+            scales = by_row([vfac_ref[(r * blocks + u) * KVH + k] for r in range(local_rows)])
+            weights.append((weight.astype(BF16).astype(F32) * scales).astype(BF16))
+        weights = jnp.concatenate(weights, axis=1)
+        summed = None
+        for r in range(local_rows):
+            one = jnp.dot(weights, vc[r, :, at_k], preferred_element_type=F32)
+            summed = one if r == 0 else jnp.where(ridx == r, one, summed)
+        summed = summed + own_weight.astype(BF16).astype(F32) * new_value
+        result = (summed / total).astype(BF16)
+        for s in range(per_head):
+            asend[k * per_head + s] = result[s * tile:(s + 1) * tile, :]
+
+    def a_copy(o, slot):
+        return remote(asend.at[o], abuf.at[slot], a_send.at[o], a_recv.at[slot], o)
+
+    others(lambda o: a_copy(o, me).start())
+    abuf[me] = asend[me]
+    for i in range(wo_parts):
+        wo_copy(i).wait()
+    others(lambda o: a_copy(o, o).wait_recv())
+    pk[...] = abuf[...].astype(F32)
+    for j in range(n):
+        for g in range(own_heads):
+            heads[j * local_rows:(j + 1) * local_rows, g * HD:(g + 1) * HD] = (
+                pk[j, g * local_rows:(g + 1) * local_rows, :]
+            )
+    attended = heads[...].astype(BF16)
+
+    def partial(block):
+        start = pl.multiple_of(block * width, width)
+        return jnp.dot(attended, wo[:, pl.ds(start, width)], preferred_element_type=F32)
+
+    def core_copy(slot):
+        return remote(core_sb.at[slot], core_rb.at[slot], core_send.at[slot], core_recv.at[slot], cpeer)
+
+    def y_copy(pos):
+        return remote(y_sb.at[pos], y_rb.at[pos], y_send.at[pos], y_recv.at[pos], ypeer)
+
+    def up_copy(pos):
+        return remote(z_sb.at[pos], up_rb.at[pos], z_send.at[pos], up_recv.at[pos], up)
+
+    def dn_copy(pos):
+        return remote(z_sb.at[pos], dn_rb.at[pos], z_send.at[pos], dn_recv.at[pos], down)
+
+    def loop_far(body):
+        def step(m, carry):
+            body(ranked(line - 1 - m))
+            return carry
+        lax.fori_loop(0, line, step, 0)
+
+    def to_core_far(pos):
+        core_sb[line + pos] = partial(at(pos, 1 - b, 1 - c)).astype(BF16)
+        core_copy(line + pos).start()
+
+    def to_pair(pos):
+        term = partial(at(pos, 1 - b, c))
+        core_copy(line + pos).wait_recv()
+        y_sb[pos] = (term + core_rb[line + pos].astype(F32)).astype(BF16)
+        y_copy(pos).start()
+
+    def to_core_near(pos):
+        core_sb[pos] = partial(at(pos, b, 1 - c)).astype(BF16)
+        core_copy(pos).start()
+
+    def to_line(pos):
+        term = partial(at(pos, b, c))
+        core_copy(pos).wait_recv()
+        term = term + core_rb[pos].astype(F32)
+        y_copy(pos).wait_recv()
+        term = term + y_rb[pos].astype(F32)
+        heads_sum[...] = term
+
+        @pl.when((pos >= a) & (a > 0))
+        def _():
+            up_copy(pos).wait_recv()
+            heads_sum[...] += up_rb[pos].astype(F32)
+
+        @pl.when((pos <= a) & (a < line - 1))
+        def _():
+            dn_copy(pos).wait_recv()
+            heads_sum[...] += dn_rb[pos].astype(F32)
+
+        @pl.when(pos > a)
+        def _():
+            z_sb[pos] = heads_sum[...].astype(BF16)
+            up_copy(pos).start()
+
+        @pl.when(pos < a)
+        def _():
+            z_sb[pos] = heads_sum[...].astype(BF16)
+            dn_copy(pos).start()
+
+        @pl.when(pos == a)
+        def _():
+            out_ref[...] = (x_ref[...].astype(F32) + heads_sum[...]).astype(BF16)
+
+    loop_far(to_core_far)
+    loop_far(to_pair)
+    loop_far(to_core_near)
+    loop_far(to_line)
+
+    def sent(pos, carry):
+        block = at(pos, b, c)
+
+        @pl.when((pos <= a) & (a < line - 1))
+        def _():
+            ag_copy(block, ag_up.at[pos], up).wait_send()
+
+        @pl.when((pos >= a) & (a > 0))
+        def _():
+            ag_copy(block, ag_dn.at[pos], down).wait_send()
+
+        ag_copy(block, ag_y.at[pos], ypeer).wait_send()
+        ag_copy(block, ag_core.at[pos], cpeer).wait_send()
+        ag_copy(at(pos, 1 - b, c), ag_core.at[line + pos], cpeer).wait_send()
+        core_copy(pos).wait_send()
+        core_copy(line + pos).wait_send()
+        y_copy(pos).wait_send()
+
+        @pl.when(pos > a)
+        def _():
+            up_copy(pos).wait_send()
+
+        @pl.when(pos < a)
+        def _():
+            dn_copy(pos).wait_send()
+        return carry
+    lax.fori_loop(0, line, sent, 0)
+
+    def sent_others(o):
+        ss_copy(o, o).wait_send()
+        q_copy(o, o).wait_send()
+        a_copy(o, o).wait_send()
+    others(sent_others)
+
+
+def fused_device(
+    n, stream, norm_gain, w_query, w_keyval, w_out, lengths, key_cache, value_cache,
+    key_scales, value_scales,
+):
+    rows, width = stream.shape
+    local_rows = lengths.shape[0]
+    span = key_cache.shape[1]
+    line = n // 4
+    qcols = w_query.shape[1]
+    tile = (qcols // HD + 1) * local_rows
+    qrows = n // KVH * tile
+    half = HD // 2
+    freq = jnp.exp(jnp.arange(half, dtype=F32) * (-2.0 * math.log(rope_base) / HD))
+    angle = lengths.astype(F32)[:, None] * freq
+    cosine, sine = jnp.cos(angle), jnp.sin(angle)
+    cosine = jnp.tile(jnp.concatenate([cosine, cosine], axis=1), (qrows // local_rows, 1))
+    sine = jnp.tile(jnp.concatenate([-sine, sine], axis=1), (qrows // local_rows, 1))
+    kfac = jnp.exp2(key_scales.astype(F32)).astype(BF16).astype(F32).reshape(-1)
+    vfac = jnp.exp2(value_scales.astype(F32)).astype(BF16).astype(F32).reshape(-1)
+    vmem = pl.BlockSpec(memory_space=pltpu.VMEM)
+    smem = pl.BlockSpec(memory_space=pltpu.SMEM)
+    hbm = pl.BlockSpec(memory_space=pl.ANY)
+    kv_cols = w_keyval.shape[1]
+    block = (rows, width)
+    dma = pltpu.SemaphoreType.DMA
+    return pl.pallas_call(
+        functools.partial(fused_kernel, n, rows, width, local_rows, span),
+        out_shape=jax.ShapeDtypeStruct(block, BF16),
+        in_specs=[vmem] * 4 + [smem] * 3 + [hbm] * 5,
+        out_specs=vmem,
+        scratch_shapes=[
+            pltpu.VMEM(w_query.shape, BF16),
+            pltpu.VMEM((kv_cols, n * width), BF16),
+            pltpu.VMEM(w_out.shape, BF16),
+            pltpu.VMEM(key_cache.shape, BF16),
+            pltpu.VMEM(value_cache.shape, BF16),
+            pltpu.VMEM((n,) + block, BF16),
+            pltpu.VMEM((8, 128), F32),
+            pltpu.VMEM((n, 8, 128), F32),
+            pltpu.VMEM((rows, qcols), F32),
+            pltpu.VMEM((rows, kv_cols), F32),
+            pltpu.VMEM((n, tile, HD), F32),
+            pltpu.VMEM((n, tile, HD), BF16),
+            pltpu.VMEM((n, tile, HD), BF16),
+            pltpu.VMEM((n, tile, HD), BF16),
+            pltpu.VMEM((n, tile, HD), BF16),
+            pltpu.VMEM((rows, qcols), F32),
+            pltpu.VMEM((2 * line,) + block, BF16),
+            pltpu.VMEM((2 * line,) + block, BF16),
+            pltpu.VMEM((line,) + block, BF16),
+            pltpu.VMEM((line,) + block, BF16),
+            pltpu.VMEM((line,) + block, BF16),
+            pltpu.VMEM((line,) + block, BF16),
+            pltpu.VMEM((line,) + block, BF16),
+            pltpu.VMEM(block, F32),
+            dma((n,)), dma((4,)), dma((3,)),
+            dma((n,)), dma((line,)), dma((line,)), dma((line,)), dma((2 * line,)),
+            dma((n,)), dma((n,)), dma((n,)), dma((n,)), dma((n,)), dma((n,)),
+            dma((2 * line,)), dma((2 * line,)), dma((line,)), dma((line,)), dma((line,)),
+            dma((line,)), dma((line,)),
+        ],
+        compiler_params=pltpu.CompilerParams(
+            collective_id=0, has_side_effects=True, vmem_limit_bytes=52 * 2**20
+        ),
+        cost_estimate=pl.CostEstimate(
+            flops=4 * rows * w_query.size, bytes_accessed=4 * w_query.size, transcendentals=0
+        ),
+    )(
+        stream, norm_gain.reshape(1, -1), cosine, sine, lengths, kfac, vfac,
+        w_query, w_keyval.T, w_out, key_cache, value_cache,
+    )
+
+
+def per_device(n, *args):
+    stream, _, w_query, w_keyval, _, lengths, key_cache, *_ = args
+    rows, width = stream.shape
+    local_rows = lengths.shape[0]
+    qcols, kv_cols = w_query.shape[1], w_keyval.shape[1]
+    tiles = (
+        n % 4 == 0 and n % KVH == 0 and width % 128 == 0 and qcols % HD == 0
+        and HD % kv_cols == 0 and rows % 16 == 0 and rows <= 128
+        and (qcols // HD + 1) * local_rows % 16 == 0
+        and key_cache.shape[1] // 128 == args[8].shape[1]
+    )
+    return fused_device(n, *args) if tiles else plain_device(*args)
+
+
 def solution(mesh):
     return jax.shard_map(
-        per_device,
+        functools.partial(per_device, mesh.shape["out"]),
         mesh=mesh,
         in_specs=(
             P("groups", "out"),

time: 174 us -> 62.7 us (0.36)
  waiting for transfers between devices: 112 us -> 0 us
  Pallas kernels: 0 us -> 55.5 us
  matrix products: 19.8 us -> 0 us
  between operations: 13.6 us -> 0.05 us
  starting transfers between devices: 9.79 us -> 0 us
  blocking collectives: 9.34 us -> 0 us
  other arithmetic: 6.88 us -> 2.28 us
  local copies, waits for them, and re-layouts: 2.16 us -> 4.59 us
    reduce_scatter x1 -> x0, waiting for transfers between devices: 63.6 us -> none  [per_device(): lax.psum_scatter(partial_terms, 'out', scatter_dimension=1, tiled=True)]
    pallas_call x0 -> x1, Pallas kernels: none -> 55.5 us  [fused_device(): pl.pallas_call(functools.partial(fused_kernel, n, rows, width, local_rows...]
    all_gather x1 -> x0, waiting for transfers between devices: 41.3 us -> none  [per_device(): lax.all_gather(stream, 'out', axis=1, tiled=True).astype(jnp.float32)]
    dot_general x6 -> x0, matrix products: 19.8 us -> none  [the longest x1 7.11 us: per_device(): partial_terms = jnp.dot(heads, w_out, preferred_element_type=jnp.float32)]
    all_to_all x2 -> x0, starting transfers between devices: 9.75 us -> none  [the longest x1 6.01 us: per_device(): lax.all_to_all(q_local, 'out', split_axis=0, concat_axis=1, tiled=True)]
    all_to_all x1 -> x0, blocking collectives: 9.34 us -> none  [per_device(): lax.all_to_all(attended, 'out', split_axis=1, concat_axis=0, tiled=True)]
    all_to_all x2 -> x0, waiting for transfers between devices: 6.33 us -> none  [the longest x1 6.33 us: per_device(): lax.all_to_all(q_local, 'out', split_axis=0, concat_axis=1, tiled=True)]
    unnamed x10 -> x9, local copies, waits for them, and re-layouts: 0.79 us -> 4.39 us
  transfers between devices with their start and end apart: 4 -> 0, of which waited for: 3 -> 0; matrix products, arithmetic and copies ran while one was open for 5% -> 0% of each run, Pallas kernels for 0% -> 0%
where the time goes in v1:
time: 62.7 us; the launch traced here: 62.4 us
  Pallas kernels  55.5 us (89%)
  local copies, waits for them, and re-layouts  4.59 us (7%)
  other arithmetic  2.28 us (4%)
    pallas_call x1, Pallas kernels, fused_device(): pl.pallas_call(functools.partial(fused_kernel, n, rows, width, local_rows...  55.5 us
    unnamed x9, local copies, waits for them, and re-layouts  4.39 us

profile of v1, /device:TPU:0, one launch (start us, length us, event | category | flops | bytes accessed | tf_op | source)
XLA Modules:
  0.0 62.4 jit_solution(8255427774899760862)
XLA Ops:
  0.0 0.7 %convert_element_type.17 = f32[4]{0:T(128)S(1)} convert(s32[4]{0:T(128)} %len_ref.1) | non-fusion elementwise | flops 4 | bytes 32 | tf_op jit(solution)/shard_map/convert_element_type | solution.py:499
  0.7 0.1 fusion.2
  0.8 0.1 pad_maximum_fusion
  0.9 0.7 %fusion = f32[4,4,4]{2,1,0:T(4,128)S(1)} fusion(s32[4,4,4]{2,1,0:T(4,128)} %param.18), kind=kLoop, calls=%fused_computation.2 | loop fusion | flops 256 | bytes 512 | tf_op jit(solution)/shard_map/reshape | solution.py:503
  1.6 0.1 reshape.33.kfac_ref
  1.7 0.7 %fusion.1 = f32[4,4,4]{2,1,0:T(4,128)S(1)} fusion(s32[4,4,4]{2,1,0:T(4,128)} %param.19), kind=kLoop, calls=%fused_computation.3 | loop fusion | flops 256 | bytes 512 | tf_op jit(solution)/shard_map/reshape | solution.py:504
  2.4 0.1 reshape.35.vfac_ref
  2.5 0.0 copy-start
  2.5 1.4 %copy-done = bf16[12288,64]{0,1:T(8,128)(2,1)S(1)} copy-done((bf16[12288,64]{0,1:T(8,128)(2,1)S(1)}, bf16[12288,64]{0,1:T(8,128)(2,1)}, u32[]{:S(2)}) %copy-start) | copy-done | bytes 1572888
  3.9 0.0 copy-start.1
  3.9 0.9 %copy-done.1 = bf16[64,768]{1,0:T(8,128)(2,1)S(1)} copy-done((bf16[64,768]{1,0:T(8,128)(2,1)S(1)}, bf16[64,768]{1,0:T(8,128)(2,1)}, u32[]{:S(2)}) %copy-start.1) | copy-done | bytes 98328
  4.8 0.0 copy-start.2
  4.8 0.8 %copy-done.2 = f32[12288]{0:T(1024)S(1)} copy-done((f32[12288]{0:T(1024)S(1)}, f32[12288]{0:T(1024)}, u32[]{:S(2)}) %copy-start.2) | copy-done | bytes 49176
  5.6 0.0 copy-start.3
  5.6 0.7 %copy-done.3 = s32[4]{0:T(128)S(1)} copy-done((s32[4]{0:T(128)S(1)}, s32[4]{0:T(128)}, u32[]{:S(2)}) %copy-start.3) | copy-done | bytes 40
  6.3 55.5 %shard_map.100 = bf16[64,768]{1,0:T(8,128)(2,1)S(1)} custom-call(bf16[64,768]{1,0:T(8,128)(2,1)S(1)} %copy-done.1, f32[1,12288]{1,0:T(1,128)S(1)} %bitcast.7, f32[64,128]{1,0:T(8,128)S(1)} %bitcast.5, f32[64,128]{1,0:T(8,128)S(1)} %bitcast.6, s32[4]{0:T(128)S(1)} %copy-done.3, f32[64]{0:T(128)S(1)} %reshape.33.kfac_ref, f32[64]{0:T(128)S(1)} %reshape.35.vfac_ref, ...), custom_call_target="tpu_custom_call" | custom-call | flops 1207959552 | bytes 18874368 | tf_op jit(solution)/shard_map/pallas_call | solution.py:511
  61.8 0.6 %copy.12 = bf16[64,768]{1,0:T(8,128)(2,1)} copy(bf16[64,768]{1,0:T(8,128)(2,1)S(1)} %shard_map.100) | data formatting | bytes 196608
  (3 shorter events, 0.0 us)
Async XLA Ops:
  2.5 1.4 %copy-start = (bf16[12288,64]{0,1:T(8,128)(2,1)S(1)}, bf16[12288,64]{0,1:T(8,128)(2,1)}, u32[]{:S(2)}) copy-start(bf16[12288,64]{0,1:T(8,128)(2,1)} %param.13) | copy-start | bytes 4718596
  3.9 0.9 %copy-start.1 = (bf16[64,768]{1,0:T(8,128)(2,1)S(1)}, bf16[64,768]{1,0:T(8,128)(2,1)}, u32[]{:S(2)}) copy-start(bf16[64,768]{1,0:T(8,128)(2,1)} %x_ref.1) | copy-start | bytes 294916
  4.8 0.8 %copy-start.2 = (f32[12288]{0:T(1024)S(1)}, f32[12288]{0:T(1024)}, u32[]{:S(2)}) copy-start(f32[12288]{0:T(1024)} %param.11) | copy-start | bytes 147460
  5.6 0.7 %copy-start.3 = (s32[4]{0:T(128)S(1)}, s32[4]{0:T(128)}, u32[]{:S(2)}) copy-start(s32[4]{0:T(128)} %len_ref.1) | copy-start | bytes 52

commit v2 on v1

--- a/solution.py
+++ b/solution.py
@@ -112,10 +112,10 @@
 
 def fused_kernel(
     n, rows, width, local_rows, span,
-    x_ref, gain_ref, cos_ref, sin_ref, len_ref, kfac_ref, vfac_ref,
-    wq_hbm, wkv_hbm, wo_hbm, kc_hbm, vc_hbm,
+    len_ref, ks_ref, vs_ref,
+    x_hbm, gain_hbm, wq_hbm, wkv_hbm, wo_hbm, kc_hbm, vc_hbm,
     out_ref,
-    wq, wkv, wo, kc, vc, xbuf, ssend, sbuf, accq, acckv, pk, qsend, qbuf, asend, abuf, heads,
+    x_ref, gain_ref, cos_ref, sin_ref, kfac, vfac, wq, wkv, wo, kc, vc, xbuf, ssend, sbuf, accq, acckv, pk, qsend, qbuf, asend, abuf, heads,
     core_sb, core_rb, y_sb, y_rb, z_sb, up_rb, dn_rb, heads_sum,
     wq_sem, wo_sem, w_sem,
     ag_recv, ag_up, ag_dn, ag_y, ag_core,
@@ -169,6 +169,11 @@
     kc_copy = pltpu.make_async_copy(kc_hbm, kc, w_sem.at[1])
     vc_copy = pltpu.make_async_copy(vc_hbm, vc, w_sem.at[2])
 
+    x_copy = pltpu.make_async_copy(x_hbm, x_ref, w_sem.at[3])
+    gain_copy = pltpu.make_async_copy(gain_hbm, gain_ref, w_sem.at[4])
+    x_copy.start()
+    gain_copy.start()
+
     barrier = pltpu.get_barrier_semaphore()
 
     def others(body):
@@ -190,6 +195,7 @@
     for i in range(wo_parts):
         wo_copy(i).start()
 
+    x_copy.wait()
     xbuf[me] = x_ref[...]
     xf = x_ref[...].astype(F32)
     square = jnp.sum(xf * xf, axis=1, keepdims=True)
@@ -200,37 +206,70 @@
     accq[...] = jnp.zeros_like(accq)
     acckv[...] = jnp.zeros_like(acckv)
 
+    ridx = lax.broadcasted_iota(jnp.int32, (qrows, 128), 0) % local_rows
+    pick = lax.broadcasted_iota(jnp.int32, (qrows, tile), 0) % local_rows
+    pick = pick + own_heads * local_rows == lax.broadcasted_iota(jnp.int32, (qrows, tile), 1)
+    pick = pick.astype(F32).astype(BF16)
+    blocks = span // 128
+    few = lax.broadcasted_iota(jnp.int32, (8, 128), 0) % local_rows
+    lane8 = lax.broadcasted_iota(jnp.int32, (8, 128), 1)
+
+    def by_row(values):
+        res = jnp.full((8, 128), values[0])
+        for r in range(1, local_rows):
+            res = jnp.where(few == r, values[r], res)
+        return res
+
+    def tall(v):
+        return jnp.concatenate([v] * (qrows // 8), axis=0)
+
+    limit8 = by_row([len_ref[r] for r in range(local_rows)])
+    freq = jnp.exp((lane8 % (HD // 2)).astype(F32) * (-2.0 * math.log(rope_base) / HD))
+    angle = limit8.astype(F32) * freq
+    cos_ref[...] = jnp.cos(angle)
+    sin_ref[...] = jnp.where(lane8 < HD // 2, -1.0, 1.0) * jnp.sin(angle)
+    for k in range(KVH):
+        for u in range(blocks):
+            for ref, table in ((ks_ref, kfac), (vs_ref, vfac)):
+                power = by_row([ref[r, u, k] for r in range(local_rows)]).astype(F32)
+                table[k * blocks + u] = jnp.exp2(power).astype(BF16).astype(F32)
+
     pl.semaphore_wait(barrier, n - 1)
 
-    def ag_copy(block, ssem, to):
-        return remote(xbuf.at[block], xbuf.at[block], ssem, ag_recv.at[block], to)
-
-    def ag_wait(block):
-        ag_copy(block, ag_core.at[0], cpeer).wait_recv()
-
-    def spread_line(pos):
+    half_rows = rows // 2
+
+    def ag_copy(block, h, ssem, to):
+        part = xbuf.at[block, pl.ds(h * half_rows, half_rows)]
+        return remote(part, part, ssem, ag_recv.at[2 * block + h], to)
+
+    def ag_wait(block, h):
+        ag_copy(block, h, ag_core.at[0], cpeer).wait_recv()
+
+    def spread_line(pos, h):
         block = at(pos, b, c)
 
         @pl.when((pos <= a) & (a < line - 1))
         def _():
-            ag_copy(block, ag_up.at[pos], up).start()
+            ag_copy(block, h, ag_up.at[2 * pos + h], up).start()
 
         @pl.when((pos >= a) & (a > 0))
         def _():
-            ag_copy(block, ag_dn.at[pos], down).start()
-
-        ag_copy(block, ag_y.at[pos], ypeer).start()
-        ag_copy(block, ag_core.at[pos], cpeer).start()
+            ag_copy(block, h, ag_dn.at[2 * pos + h], down).start()
+
+        ag_copy(block, h, ag_y.at[2 * pos + h], ypeer).start()
+        ag_copy(block, h, ag_core.at[2 * pos + h], cpeer).start()
 
     def ss_copy(o, slot):
         return remote(ssend, sbuf.at[slot], ss_send.at[o], ss_recv.at[slot], o)
 
     others(lambda o: ss_copy(o, me).start())
-    spread_line(a)
+    for h in range(2):
+        spread_line(a, h)
     others(lambda o: ss_copy(o, o).wait_recv())
     total_sq = jnp.sum(sbuf[...], axis=0)[0:1, :]
     column = jnp.transpose(jnp.broadcast_to(total_sq, (128, 128)))[0:rows, 0:1]
     scale = lax.rsqrt(column * (1.0 / (n * width)) + norm_eps)
+    gain_copy.wait()
     wkv_copy.wait()
 
     def project(block):
@@ -242,37 +281,48 @@
             normed, wkv[:, pl.ds(start, width)], CONTRACT_LAST, preferred_element_type=F32
         )
 
+    def take_line(m, h):
+        @pl.when(m < line)
+        def _():
+            pos = ranked(m)
+            ag_wait(at(pos, b, c), h)
+            spread_line(pos, h)
+
+    def take_pair(m, h):
+        pos = ranked(m)
+        block = at(pos, 1 - b, c)
+        ag_wait(block, h)
+        ag_copy(block, h, ag_core.at[2 * (line + pos) + h], cpeer).start()
+
     project(me)
 
     def gather_step(m, carry):
+        take_line(m, 0)
+        take_pair(m - 1, 0)
+        cblock = at(ranked(m - 1), b, 1 - c)
+        for h in range(2):
+            ag_wait(cblock, h)
+        project(cblock)
+        take_line(m, 1)
+        take_pair(m - 1, 1)
+        project(at(ranked(m - 1), 1 - b, c))
+
         @pl.when(m < line)
         def _():
-            pos = ranked(m)
-            ag_wait(at(pos, b, c))
-            spread_line(pos)
-
-        prev = ranked(m - 1)
-        yblock = at(prev, 1 - b, c)
-        ag_wait(yblock)
-        ag_copy(yblock, ag_core.at[line + prev], cpeer).start()
-
-        @pl.when(m < line)
-        def _():
             project(at(ranked(m), b, c))
 
-        project(yblock)
-        cblock = at(prev, b, 1 - c)
-        ag_wait(cblock)
-        project(cblock)
+        @pl.when(m > 1)
+        def _():
+            block = at(ranked(m - 2), 1 - b, 1 - c)
+            for h in range(2):
+                ag_wait(block, h)
+            project(block)
         return carry
     lax.fori_loop(1, line + 1, gather_step, 0)
-
-    def gather_last(m, carry):
-        block = at(ranked(m), 1 - b, 1 - c)
-        ag_wait(block)
-        project(block)
-        return carry
-    lax.fori_loop(0, line, gather_last, 0)
+    last = at(ranked(line - 1), 1 - b, 1 - c)
+    for h in range(2):
+        ag_wait(last, h)
+    project(last)
 
     kv_cols = wkv.shape[0]
     pk[...] = jnp.zeros_like(pk)
@@ -291,21 +341,9 @@
     others(lambda o: q_copy(o, me).start())
     qbuf[me] = qsend[me]
 
-    ridx = lax.broadcasted_iota(jnp.int32, (qrows, 128), 0) % local_rows
-    pick = lax.broadcasted_iota(jnp.int32, (qrows, tile), 0) % local_rows
-    pick = pick + own_heads * local_rows == lax.broadcasted_iota(jnp.int32, (qrows, tile), 1)
-    pick = pick.astype(F32).astype(BF16)
-    blocks = span // 128
-
-    def by_row(values):
-        res = jnp.full((qrows, 128), values[0])
-        for r in range(1, local_rows):
-            res = jnp.where(ridx == r, values[r], res)
-        return res
-
-    limit = by_row([len_ref[r] for r in range(local_rows)])
+    limit = tall(limit8)
     lane = lax.broadcasted_iota(jnp.int32, (qrows, 128), 1)
-    cosine, sine = cos_ref[...], sin_ref[...]
+    cosine, sine = tall(cos_ref[...]), tall(sin_ref[...])
 
     def rotated(v):
         return (v * cosine + pltpu.roll(v, HD // 2, 1) * sine).astype(BF16)
@@ -338,7 +376,7 @@
             score = cut if r == 0 else [jnp.where(ridx == r, x, y) for x, y in zip(cut, score)]
         top = own
         for u in range(blocks):
-            scales = by_row([kfac_ref[(r * blocks + u) * KVH + k] for r in range(local_rows)])
+            scales = tall(kfac[k * blocks + u])
             score[u] = jnp.where(lane + 128 * u < limit, score[u] * scales * factor, -jnp.inf)
             top = jnp.maximum(top, jnp.max(score[u], axis=1, keepdims=True))
         own_weight = jnp.exp(own - top)
@@ -347,7 +385,7 @@
         for u in range(blocks):
             weight = jnp.exp(score[u] - top)
             total = total + jnp.sum(weight, axis=1, keepdims=True)
-            scales = by_row([vfac_ref[(r * blocks + u) * KVH + k] for r in range(local_rows)])
+            scales = tall(vfac[k * blocks + u])
             weights.append((weight.astype(BF16).astype(F32) * scales).astype(BF16))
         weights = jnp.concatenate(weights, axis=1)
         summed = None
@@ -443,25 +481,40 @@
         def _():
             out_ref[...] = (x_ref[...].astype(F32) + heads_sum[...]).astype(BF16)
 
-    loop_far(to_core_far)
-    loop_far(to_pair)
+    def far(m):
+        return ranked(line - 1 - m)
+
+    to_core_far(far(0))
+
+    def pair_step(m, carry):
+        @pl.when(m < line - 1)
+        def _():
+            to_core_far(far(m + 1))
+        to_pair(far(m))
+        return carry
+    lax.fori_loop(0, line, pair_step, 0)
     loop_far(to_core_near)
     loop_far(to_line)
 
+    def sent_gather(i, carry):
+        pos, h = i // 2, i % 2
+        block = at(pos, b, c)
+
+        @pl.when((pos <= a) & (a < line - 1))
+        def _():
+            ag_copy(block, h, ag_up.at[2 * pos + h], up).wait_send()
+
+        @pl.when((pos >= a) & (a > 0))
+        def _():
+            ag_copy(block, h, ag_dn.at[2 * pos + h], down).wait_send()
+
+        ag_copy(block, h, ag_y.at[2 * pos + h], ypeer).wait_send()
+        ag_copy(block, h, ag_core.at[2 * pos + h], cpeer).wait_send()
+        ag_copy(at(pos, 1 - b, c), h, ag_core.at[2 * (line + pos) + h], cpeer).wait_send()
+        return carry
+    lax.fori_loop(0, 2 * line, sent_gather, 0)
+
     def sent(pos, carry):
-        block = at(pos, b, c)
-
-        @pl.when((pos <= a) & (a < line - 1))
-        def _():
-            ag_copy(block, ag_up.at[pos], up).wait_send()
-
-        @pl.when((pos >= a) & (a > 0))
-        def _():
-            ag_copy(block, ag_dn.at[pos], down).wait_send()
-
-        ag_copy(block, ag_y.at[pos], ypeer).wait_send()
-        ag_copy(block, ag_core.at[pos], cpeer).wait_send()
-        ag_copy(at(pos, 1 - b, c), ag_core.at[line + pos], cpeer).wait_send()
         core_copy(pos).wait_send()
         core_copy(line + pos).wait_send()
         y_copy(pos).wait_send()
@@ -493,15 +546,6 @@
     line = n // 4
     qcols = w_query.shape[1]
     tile = (qcols // HD + 1) * local_rows
-    qrows = n // KVH * tile
-    half = HD // 2
-    freq = jnp.exp(jnp.arange(half, dtype=F32) * (-2.0 * math.log(rope_base) / HD))
-    angle = lengths.astype(F32)[:, None] * freq
-    cosine, sine = jnp.cos(angle), jnp.sin(angle)
-    cosine = jnp.tile(jnp.concatenate([cosine, cosine], axis=1), (qrows // local_rows, 1))
-    sine = jnp.tile(jnp.concatenate([-sine, sine], axis=1), (qrows // local_rows, 1))
-    kfac = jnp.exp2(key_scales.astype(F32)).astype(BF16).astype(F32).reshape(-1)
-    vfac = jnp.exp2(value_scales.astype(F32)).astype(BF16).astype(F32).reshape(-1)
     vmem = pl.BlockSpec(memory_space=pltpu.VMEM)
     smem = pl.BlockSpec(memory_space=pltpu.SMEM)
     hbm = pl.BlockSpec(memory_space=pl.ANY)
@@ -511,9 +555,15 @@
     return pl.pallas_call(
         functools.partial(fused_kernel, n, rows, width, local_rows, span),
         out_shape=jax.ShapeDtypeStruct(block, BF16),
-        in_specs=[vmem] * 4 + [smem] * 3 + [hbm] * 5,
+        in_specs=[smem] * 3 + [hbm] * 7,
         out_specs=vmem,
         scratch_shapes=[
+            pltpu.VMEM(block, BF16),
+            pltpu.VMEM((1, n * width), F32),
+            pltpu.VMEM((8, HD), F32),
+            pltpu.VMEM((8, HD), F32),
+            pltpu.VMEM((KVH * (span // 128), 8, 128), F32),
+            pltpu.VMEM((KVH * (span // 128), 8, 128), F32),
             pltpu.VMEM(w_query.shape, BF16),
             pltpu.VMEM((kv_cols, n * width), BF16),
             pltpu.VMEM(w_out.shape, BF16),
@@ -538,20 +588,20 @@
             pltpu.VMEM((line,) + block, BF16),
             pltpu.VMEM((line,) + block, BF16),
             pltpu.VMEM(block, F32),
-            dma((n,)), dma((4,)), dma((3,)),
-            dma((n,)), dma((line,)), dma((line,)), dma((line,)), dma((2 * line,)),
+            dma((n,)), dma((4,)), dma((5,)),
+            dma((2 * n,)), dma((2 * line,)), dma((2 * line,)), dma((2 * line,)), dma((4 * line,)),
             dma((n,)), dma((n,)), dma((n,)), dma((n,)), dma((n,)), dma((n,)),
             dma((2 * line,)), dma((2 * line,)), dma((line,)), dma((line,)), dma((line,)),
             dma((line,)), dma((line,)),
         ],
         compiler_params=pltpu.CompilerParams(
-            collective_id=0, has_side_effects=True, vmem_limit_bytes=52 * 2**20
+            collective_id=0, has_side_effects=True, vmem_limit_bytes=62 * 2**20
         ),
         cost_estimate=pl.CostEstimate(
             flops=4 * rows * w_query.size, bytes_accessed=4 * w_query.size, transcendentals=0
         ),
     )(
-        stream, norm_gain.reshape(1, -1), cosine, sine, lengths, kfac, vfac,
+        lengths, key_scales, value_scales, stream, norm_gain.reshape(1, -1),
         w_query, w_keyval.T, w_out, key_cache, value_cache,
     )
 
@@ -563,7 +613,8 @@
     qcols, kv_cols = w_query.shape[1], w_keyval.shape[1]
     tiles = (
         n % 4 == 0 and n % KVH == 0 and width % 128 == 0 and qcols % HD == 0
-        and HD % kv_cols == 0 and rows % 16 == 0 and rows <= 128
+        and HD % kv_cols == 0 and rows % 32 == 0 and rows <= 128
+        and 8 % local_rows == 0
         and (qcols // HD + 1) * local_rows % 16 == 0
         and key_cache.shape[1] // 128 == args[8].shape[1]
     )

time: 62.7 us -> 57.4 us (0.915)
  local copies, waits for them, and re-layouts: 4.59 us -> 1.54 us
  other arithmetic: 2.28 us -> 0 us
    unnamed x9 -> x1, local copies, waits for them, and re-layouts: 4.39 us -> 1.54 us
    reshape x2 -> x0, other arithmetic: 1.42 us -> none  [the longest x1 0.71 us: fused_device(): kfac = jnp.exp2(key_scales.astype(F32)).astype(BF16).astype(F32).reshape(-1)]
    convert_element_type x1 -> x0, other arithmetic: 0.66 us -> none  [fused_device(): angle = lengths.astype(F32)[:, None] * freq]
where the time goes in v2:
time: 57.4 us; the launch traced here: 56.9 us
  Pallas kernels  55.3 us (96%)
  local copies, waits for them, and re-layouts  1.54 us (3%)
    pallas_call x1, Pallas kernels, fused_device(): pl.pallas_call(functools.partial(fused_kernel, n, rows, width, local_rows...  55.3 us
    unnamed x1, local copies, waits for them, and re-layouts  1.54 us

profile of v2, /device:TPU:0, one launch (start us, length us, event | category | flops | bytes accessed | tf_op | source)
XLA Modules:
  0.0 56.9 jit_solution(7894673993143434665)
XLA Ops:
  0.0 55.3 %shard_map.100 = bf16[64,768]{1,0:T(8,128)(2,1)} custom-call(s32[4]{0:T(128)} %len_ref.1, s32[4,4,4]{2,1,0:T(4,128)} %ks_ref.1, s32[4,4,4]{2,1,0:T(4,128)} %vs_ref.1, bf16[64,768]{1,0:T(8,128)(2,1)} %x_hbm.1, f32[1,12288]{1,0:T(1,128)} %bitcast.3, bf16[12288,384]{1,0:T(8,128)(2,1)} %wq_hbm.1, bf16[64,12288]{1,0:T(8,128)(2,1)} %bitcast.2, ...), custom_call_target="tpu_custom_call" | custom-call | flops 1207959552 | bytes 18874368 | tf_op jit(solution)/shard_map/pallas_call | solution.py:555
  55.3 1.5 %copy.12 = bf16[64,768]{1,0:T(8,128)(2,1)} copy(bf16[64,768]{1,0:T(8,128)(2,1)} %shard_map.100) | data formatting | bytes 196608
